TPU v7x, 512 devices: a whole 4x4x16 slice. The times are simulated.
512 devices in a mesh: ens: 8 (over z_lo, core), sp: 64 (over y, z_hi, x).
Axes of the slice: x: 4, y: 4, z: 16 (z_hi: 4, z_lo: 4; z = z_hi * 4 + z_lo), core: 2. Of those that a mesh axis runs over, the one named last changes fastest.
Arguments:
- tokens: bfloat16 [8, 128, 384, 768], P('ens', 'sp'), may hold values from -6 to 6
- cotangent: bfloat16 [8, 128, 384, 768], P('ens', 'sp'), may hold values from -6 to 6
- w_first: bfloat16 [768, 192], replicated, may hold values from -0.4375 to 0.4375
- b_first: bfloat16 [2, 768], replicated, may hold values from -3 to 3
- w_second: bfloat16 [768, 192], replicated, may hold values from -0.4375 to 0.4375
- b_second: bfloat16 [2, 768], replicated, may hold values from -3 to 3
Outputs:
- grad_tokens: bfloat16 [8, 128, 384, 768], P('ens', 'sp')
- grad_w_first: float32 [768, 192], P('sp')
- grad_b_first: float32 [2, 768], P(None, 'sp')
- grad_w_second: float32 [768, 192], P('sp')
- grad_b_second: float32 [2, 768], P(None, 'sp')
All inputs are finite; a program needn't handle non-finite values.
Results may differ from a plain program's by a relative error of at most 0.022.
Values may be sent and summed in bfloat16 or wider, within the bound.
A program may use at most 64 MiB of HBM per device.

v0:
```python
import jax
import jax.numpy as jnp
from jax import lax
from jax.sharding import PartitionSpec as P

C = 768
NB = 8
BS = 96
KW = 128


shrink_level = 0.01


def lon_tables(modes, points):
    wave = jnp.arange(modes, dtype=jnp.int32)[:, None]
    place = jnp.arange(points, dtype=jnp.int32)[None, :]
    angle = (wave * place % points).astype(jnp.float32) * (2.0 * jnp.pi / points)
    scale = 1.0 / jnp.sqrt(jnp.float32(points))
    paired = jnp.stack([jnp.cos(angle), -jnp.sin(angle)]) * scale
    doubled = jnp.where(wave == 0, 1.0, 2.0).astype(jnp.float32)
    return (paired, paired * doubled)


def lat_table(count):
    wave = jnp.arange(count, dtype=jnp.int32)[:, None]
    place = jnp.arange(count, dtype=jnp.int32)[None, :]
    angle = (wave * place % count).astype(jnp.float32) * (2.0 * jnp.pi / count)
    scale = 1.0 / jnp.sqrt(jnp.float32(count))
    cosine = jnp.cos(angle) * scale
    sine = jnp.sin(angle) * scale
    return jnp.stack([jnp.stack([cosine, sine], axis=1), jnp.stack([-sine, cosine], axis=1)])


def product(form, left, right):
    return jnp.einsum(
        form, left, right, precision=lax.Precision.HIGHEST, preferred_element_type=jnp.float32
    )


def complex_mix(left, weight):
    rows = left.shape[1]
    mixed = product("prnb,nbq->prnq", left.reshape(2, rows, NB, BS), weight.reshape(NB, BS, 2 * BS))
    real_part = mixed[0, :, :, :BS] - mixed[1, :, :, BS:]
    imag_part = mixed[0, :, :, BS:] + mixed[1, :, :, :BS]
    return jnp.stack([real_part, imag_part]).reshape(2, rows, C)


def pair_grads(grad):
    rows = grad.shape[1]
    split = grad.reshape(2, rows, NB, BS)
    return jnp.stack(
        [
            jnp.concatenate([split[0], split[1]], axis=-1),
            jnp.concatenate([split[1], -split[0]], axis=-1),
        ]
    )


def back_mix(paired, weight):
    rows = paired.shape[1]
    return product("prnq,nbq->prnb", paired, weight.reshape(NB, BS, 2 * BS)).reshape(2, rows, C)


def weight_grad(left, paired):
    rows = left.shape[1]
    return product("prnb,prnq->nbq", left.reshape(2, rows, NB, BS), paired).reshape(C, 2 * BS)


def forward_mlp(spectrum, w_first, b_first, w_second, b_second):
    first_pre = complex_mix(spectrum, w_first) + b_first.astype(jnp.float32)[:, None, :]
    first_out = jnp.maximum(first_pre, 0.0)
    second_pre = complex_mix(first_out, w_second) + b_second.astype(jnp.float32)[:, None, :]
    return (first_pre, first_out, second_pre)


def shards(tokens, cotangent, w_first, b_first, w_second, b_second):
    field = tokens[0]
    grad_out = cotangent[0]
    lat_dev, points, chans = field.shape
    parts = lax.axis_size("sp")
    height = lat_dev * parts
    local_modes = KW // parts
    count = height * local_modes
    fwd_exact, inv_exact = lon_tables(KW, points)
    lat_exact = lat_table(height)
    lon_fwd = fwd_exact.astype(jnp.bfloat16)
    lon_inv = inv_exact.astype(jnp.bfloat16)
    lat_tab = lat_exact.astype(jnp.bfloat16)
    lon_spec = product("pkw,hwc->hpkc", fwd_exact, field)
    spec_full = product(
        "pmqh,hqkc->pmkc",
        lat_exact,
        lax.all_to_all(lon_spec, "sp", split_axis=2, concat_axis=0, tiled=True),
    )
    spectrum = spec_full.reshape(2, count, chans)
    first_pre, first_out, second_pre = forward_mlp(spectrum, w_first, b_first, w_second, b_second)
    cot_lon = product("pkw,hwc->hpkc", lon_inv, grad_out).astype(jnp.bfloat16)
    cot_full = product(
        "pmqh,hqkc->pmkc",
        lat_tab,
        lax.all_to_all(cot_lon, "sp", split_axis=2, concat_axis=0, tiled=True),
    )
    cot_spec = cot_full.reshape(2, count, chans)
    grad_second = jnp.where(jnp.abs(second_pre) > shrink_level, cot_spec, 0.0).astype(jnp.bfloat16)
    paired_second = pair_grads(grad_second)
    grad_first = jnp.where(first_pre > 0.0, back_mix(paired_second, w_second), 0.0).astype(
        jnp.bfloat16
    )
    paired_first = pair_grads(grad_first)
    grad_spec = (
        back_mix(paired_first, w_first).astype(jnp.bfloat16).reshape(2, height, local_modes, chans)
    )
    grad_lat = product("pmqh,pmkc->hqkc", lat_tab, grad_spec).astype(jnp.bfloat16)
    branch = product(
        "pkw,hpkc->hwc",
        lon_fwd,
        lax.all_to_all(grad_lat, "sp", split_axis=0, concat_axis=2, tiled=True),
    )
    grad_field = (grad_out.astype(jnp.float32) + branch).astype(jnp.bfloat16)[None]
    factor = float(lax.axis_size("ens") * height * KW) ** (-0.5)
    terms = (
        weight_grad(spectrum, paired_first) * factor,
        jnp.sum(grad_first.astype(jnp.float32), axis=1) * factor,
        weight_grad(first_out, paired_second) * factor,
        jnp.sum(grad_second.astype(jnp.float32), axis=1) * factor,
    )
    totals = lax.psum((terms[0], terms[1], terms[2], terms[3]), ("ens", "sp"))
    share = chans // parts
    offset = lax.axis_index("sp") * share
    results = (
        lax.dynamic_slice_in_dim(totals[0], offset, share, 0),
        lax.dynamic_slice_in_dim(totals[1], offset, share, 1),
        lax.dynamic_slice_in_dim(totals[2], offset, share, 0),
        lax.dynamic_slice_in_dim(totals[3], offset, share, 1),
    )
    return (grad_field, results[0], results[1], results[2], results[3])


def solution(mesh):
    return jax.shard_map(
        shards,
        mesh=mesh,
        in_specs=(P("ens", "sp", None, None), P("ens", "sp", None, None), P(), P(), P(), P()),
        out_specs=(
            P("ens", "sp", None, None),
            P("sp", None),
            P(None, "sp"),
            P("sp", None),
            P(None, "sp"),
        ),
        check_vma=False,
    )
```

profile of v0, /device:TPU:6, one launch (start us, length us, event | category | flops | bytes accessed | tf_op | source)
XLA Modules:
  0.0 759.3 jit_solution(1421279934790732276)
XLA Ops:
  11.7 21.2 %all-to-all-start.1 = ((bf16[2,2,128,768]{3,0,1,2:T(2,128)(2,1)}), bf16[2,2,128,768]{3,0,1,2:T(2,128)(2,1)S(1)}, u32[]{:S(2)}, u32[]{:S(2)}) async-start(bf16[2,2,128,768]{3,0,1,2:T(2,128)(2,1)} %copy.155), calls=%async_computation.1 | async-start | bytes 1572864 | tf_op jit(solution)/shard_map/all_to_all | solution.py:102
  36.8 36.6 %all-to-all-done.1 = bf16[2,2,128,768]{3,0,1,2:T(2,128)(2,1)S(1)} async-done(((bf16[2,2,128,768]{3,0,1,2:T(2,128)(2,1)}), bf16[2,2,128,768]{3,0,1,2:T(2,128)(2,1)S(1)}, u32[]{:S(2)}, u32[]{:S(2)}) %all-to-all-start.1) | async-done | bytes 786464 | tf_op jit(solution)/shard_map/all_to_all | solution.py:102
  73.4 12.7 %all-to-all-start = ((f32[2,2,128,768]{3,0,1,2:T(2,128)}), f32[2,2,128,768]{3,0,1,2:T(2,128)S(1)}, u32[]{:S(2)}, u32[]{:S(2)}) async-start(f32[2,2,128,768]{3,0,1,2:T(2,128)} %copy.143), calls=%async_computation | async-start | bytes 3145728 | tf_op jit(solution)/shard_map/all_to_all | solution.py:94
  93.2 34.7 %all-to-all-done = f32[2,2,128,768]{3,0,1,2:T(2,128)S(1)} async-done(((f32[2,2,128,768]{3,0,1,2:T(2,128)}), f32[2,2,128,768]{3,0,1,2:T(2,128)S(1)}, u32[]{:S(2)}, u32[]{:S(2)}) %all-to-all-start) | async-done | bytes 1572896 | tf_op jit(solution)/shard_map/all_to_all | solution.py:94
  134.8 3.0 reshape_reshape.4
  145.5 2.4 copy.177
  148.0 3.0 stack.87
  153.0 2.4 copy.178
  155.5 3.0 stack.88
  162.9 3.1 copy.152
  165.9 3.0 copy.153
  168.9 3.7 fusion.2
  177.8 2.9 copy.159
  184.4 3.1 copy.163
  191.0 3.5 fusion.1
  199.7 2.9 copy.165
  208.8 3.7 convert_element_type.116
  212.4 2.4 fusion.14
  214.9 3.1 copy.171
  217.9 42.8 %all-to-all-start.2 = ((bf16[128,2,2,768]{3,1,2,0:T(2,128)(2,1)}), bf16[128,2,2,768]{3,1,2,0:T(2,128)(2,1)}, u32[]{:S(2)}, u32[]{:S(2)}) async-start(bf16[128,2,2,768]{3,1,2,0:T(2,128)(2,1)} %copy.171), calls=%async_computation.2 | async-start | bytes 1572864 | tf_op jit(solution)/shard_map/all_to_all | solution.py:118
  263.2 4.0 fusion.17
  267.2 2.6 fusion.15
  270.6 105.0 %all-reduce = (f32[2,768]{1,0:T(2,128)S(1)}, f32[2,768]{1,0:T(2,128)S(1)}) all-reduce(f32[2,768]{1,0:T(2,128)S(1)} %mul.214, f32[2,768]{1,0:T(2,128)S(1)} %broadcast_multiply_fusion), channel_id=1, replica_groups=mesh['ens'=8,'sp'=64] {'ens','sp'}, use_global_device_ids=true, to_apply=%region_2.3 | all-reduce | flops 3072 | bytes 24576 | tf_op jit(solution)/shard_map/psum | solution.py:128
  376.8 367.8 %all-reduce.4.cloned.1.call-done = (f32[768,192]{1,0:T(8,128)}, f32[768,192]{1,0:T(8,128)}) async-done(((f32[768,192]{1,0:T(8,128)}, f32[768,192]{1,0:T(8,128)}), (f32[768,192]{1,0:T(8,128)}, f32[768,192]{1,0:T(8,128)})) %all-reduce.4.cloned.1.call-update) | async-done | bytes 1179664 | tf_op jit(solution)/shard_map/psum | solution.py:128
  (118 shorter events, 72.1 us)
Async XLA Ops:
  7.2 25.8 %copy-start = (bf16[1,2,384,768]{3,2,1,0:T(8,128)(2,1)S(1)}, bf16[1,2,384,768]{3,2,1,0:T(8,128)(2,1)}, u32[]{:S(2)}) copy-start(bf16[1,2,384,768]{3,2,1,0:T(8,128)(2,1)} %param.6) | copy-start | bytes 3538948
  8.0 25.0 %copy-start.3 = (f32[1,128,384]{2,1,0:T(8,128)}, f32[1,128,384]{2,1,0:T(8,128)S(1)}, u32[]{:S(2)}) copy-start(f32[1,128,384]{2,1,0:T(8,128)S(1)} %get-tuple-element.52) | copy-start | bytes 589828
  8.0 25.0 %copy-start.4 = (f32[1,128,384]{2,1,0:T(8,128)}, f32[1,128,384]{2,1,0:T(8,128)S(1)}, u32[]{:S(2)}) copy-start(f32[1,128,384]{2,1,0:T(8,128)S(1)} %get-tuple-element.53) | copy-start | bytes 589828
  11.7 61.7 %all-to-all-start.1 = ((bf16[2,2,128,768]{3,0,1,2:T(2,128)(2,1)}), bf16[2,2,128,768]{3,0,1,2:T(2,128)(2,1)S(1)}, u32[]{:S(2)}, u32[]{:S(2)}) async-start(bf16[2,2,128,768]{3,0,1,2:T(2,128)(2,1)} %copy.155), calls=%async_computation.1 | async-start | bytes 1572864 | tf_op jit(solution)/shard_map/all_to_all | solution.py:102
  36.8 49.3 %copy-start.25 = (bf16[2,768]{1,0:T(2,128)(2,1)S(1)}, bf16[2,768]{1,0:T(2,128)(2,1)}, u32[]{:S(2)}) copy-start(bf16[2,768]{1,0:T(2,128)(2,1)} %param.9) | copy-start | bytes 9220
  36.8 49.4 %copy-start.23 = (bf16[768,192]{0,1:T(8,128)(2,1)S(1)}, bf16[768,192]{0,1:T(8,128)(2,1)}, u32[]{:S(2)}) copy-start(bf16[768,192]{0,1:T(8,128)(2,1)} %param.8) | copy-start | bytes 884740
  73.4 54.5 %all-to-all-start = ((f32[2,2,128,768]{3,0,1,2:T(2,128)}), f32[2,2,128,768]{3,0,1,2:T(2,128)S(1)}, u32[]{:S(2)}, u32[]{:S(2)}) async-start(f32[2,2,128,768]{3,0,1,2:T(2,128)} %copy.143), calls=%async_computation | async-start | bytes 3145728 | tf_op jit(solution)/shard_map/all_to_all | solution.py:94
  86.1 3.4 copy-start.28
  87.0 52.9 %copy-start.9 = (bf16[8,96,192,1]{2,1,3,0:T(8,128)(2,1)}, bf16[8,96,192,1]{2,1,3,0:T(8,128)(2,1)S(1)}, u32[]{:S(2)}) copy-start(bf16[8,96,192,1]{2,1,3,0:T(8,128)(2,1)S(1)} %copy.192) | copy-start | bytes 884740
  129.6 2.4 copy-start.17
  129.6 2.4 copy-start.20
  155.5 4.3 copy-start.18
  155.5 4.3 copy-start.21
  155.5 4.3 copy-start.24
  158.5 1.6 copy-start.14
  202.6 2.5 copy-start.10
  206.4 6.1 copy-start.19
  206.4 6.1 copy-start.22
  217.9 529.3 %all-to-all-start.2 = ((bf16[128,2,2,768]{3,1,2,0:T(2,128)(2,1)}), bf16[128,2,2,768]{3,1,2,0:T(2,128)(2,1)}, u32[]{:S(2)}, u32[]{:S(2)}) async-start(bf16[128,2,2,768]{3,1,2,0:T(2,128)(2,1)} %copy.171), calls=%async_computation.2 | async-start | bytes 1572864 | tf_op jit(solution)/shard_map/all_to_all | solution.py:118
  260.7 483.8 %all-reduce.4.cloned.1.call-start = ((), (), s32[]{:S(2)}) async-start(), calls=%async_computation.3 | async-start | bytes 3145728 | tf_op jit(solution)/shard_map/psum | solution.py:128
  263.2 4.0 copy-start.6
  263.2 4.0 copy-start.8
  269.8 479.2 %copy-start.2 = (bf16[1,2,384,768]{2,3,1,0:T(8,128)(2,1)S(1)}, bf16[1,2,384,768]{2,3,1,0:T(8,128)(2,1)}, u32[]{:S(2)}) copy-start(bf16[1,2,384,768]{2,3,1,0:T(8,128)(2,1)} %copy.142) | copy-start | bytes 3538948
  749.0 3.2 copy-start.1
  (9 other events, 10.0 us)
Sparse Core Ops, SparseCore 0:
  269.9 474.6 all-reduce.3
where the time goes:
time: 766 us; the launch traced here: 759 us
  waiting for transfers between devices  439 us (57%)
  blocking collectives  105 us (14%)
  local copies, waits for them, and re-layouts  85.3 us (11%)
  starting transfers between devices  76.7 us (10%)
  matrix products  22.5 us (3%)
  other arithmetic  15.9 us (2%)
  between operations  14.7 us (2%)
    psum x1, waiting for transfers between devices, shards(): totals = lax.psum((terms[0], terms[1], terms[2], terms[3]), ('ens', 'sp'))  368 us
    psum x1, blocking collectives, shards(): totals = lax.psum((terms[0], terms[1], terms[2], terms[3]), ('ens', 'sp'))  105 us
    all_to_all x1, starting transfers between devices, shards(): lax.all_to_all(grad_lat, 'sp', split_axis=0, concat_axis=2, tiled=True)  42.8 us
    all_to_all x1, waiting for transfers between devices, shards(): lax.all_to_all(cot_lon, 'sp', split_axis=2, concat_axis=0, tiled=True)  36.6 us
    all_to_all x1, waiting for transfers between devices, shards(): lax.all_to_all(lon_spec, 'sp', split_axis=2, concat_axis=0, tiled=True)  34.7 us
    dot_general x12, matrix products, product(): jnp.einsum(form, left, right, precision=lax.Precision.HIGHEST, preferred_...  22.5 us
    all_to_all x1, starting transfers between devices, shards(): lax.all_to_all(cot_lon, 'sp', split_axis=2, concat_axis=0, tiled=True)  21.2 us
    another operation x8, local copies, waits for them, and re-layouts, complex_mix(): return jnp.stack([real_part, imag_part]).reshape(2, rows, C)  18.9 us
  transfers between devices with their start and end apart: 4, of which 3 were waited for; matrix products, arithmetic and copies ran while one was open for 3% of the time, Pallas kernels for 0%

commit v1 on v0

v1 whole, which is shorter than its diff:
```python
import functools

import jax
import jax.numpy as jnp
import ml_dtypes
import numpy as np
from jax import lax
from jax.experimental import pallas as pl
from jax.experimental.pallas import tpu as pltpu
from jax.sharding import PartitionSpec as P

MESH = pl.DeviceIdType.MESH
BF = jnp.bfloat16
F32 = jnp.float32
LEVEL = 0.01
CODE_SPAN = 249.0
CODE_BASE = 124.0
FACTOR = float(131072) ** (-0.5)


def constants():
    k = np.arange(128)[:, None]
    w = np.arange(384)[None, :]
    a = 2.0 * np.pi * ((k * w) % 384) / 384.0
    lon = (np.stack([np.cos(a), -np.sin(a)]) / np.sqrt(384.0)).astype(np.float32)
    lon = lon.reshape(2, 32, 4, 384).transpose(1, 0, 2, 3).reshape(256, 384)
    m = np.arange(128)[:, None]
    h = np.arange(128)[None, :]
    b = 2.0 * np.pi * ((m * h) % 128) / 128.0
    c, s = np.cos(b) / np.sqrt(128.0), np.sin(b) / np.sqrt(128.0)
    lat = np.stack([np.stack([c, s], 2), np.stack([-s, c], 2)])
    lat = lat.astype(np.float32).reshape(256, 256)

    def split(t):
        hi = t.astype(ml_dtypes.bfloat16)
        return hi, (t - hi.astype(np.float32)).astype(ml_dtypes.bfloat16)

    lon_hi, lon_lo = split(lon)
    lat_hi, lat_lo = split(lat)
    place = np.zeros((2, 2, 4, 2, 16, 384), np.float32)
    for yy in range(2):
        for z in range(4):
            for x in range(4):
                for r in range(12):
                    place[yy, z // 2, x, z % 2, r, yy * 192 + z * 48 + x * 12 + r] = 1.0
    place = place.reshape(512, 384).astype(ml_dtypes.bfloat16)
    return [lon_hi, lon_lo, np.ascontiguousarray(lon_hi.T), lat_hi, lat_lo, np.ascontiguousarray(lat_hi.T), place]


def dot(a, b):
    return lax.dot_general(a, b, (((1,), (0,)), ((), ())), preferred_element_type=F32)


def dot_t(a, b):
    return lax.dot_general(a, b, (((1,), (1,)), ((), ())), preferred_element_type=F32)


def halves(x):
    hi = x.astype(BF)
    return hi, (x - hi.astype(F32)).astype(BF)


def iota(shape, dim):
    return lax.broadcasted_iota(jnp.int32, shape, dim)


def block_of(i):
    return (i >= 96).astype(jnp.int32) + (i >= 192).astype(jnp.int32) + (i >= 288).astype(jnp.int32)


def wide(s):
    return jnp.concatenate([s, s, s], axis=1)


def kernel(
    tok, cot, w1, b1, w2, b2, lon_hi, lon_lo, lon_t, lat_hi, lat_lo, lat_t, place,
    out, out_w,
    lonbuf, send_t, send_s, recv_t, recv_s, send_c, recv_c, send_g, recv_g,
    rows, xh, xl, spec_b, first_b, mask_b, g1_b, g2_b, v1, v2, r1, r2,
    send_a, recv_a, send_b, recv_b, send_e, recv_e, ss, rs,
):
    e = lax.axis_index("ens")
    me = lax.axis_index("sp")
    half = lax.div(me, 32)
    barrier = pltpu.get_barrier_semaphore()

    def greet(i, carry):
        pl.semaphore_signal(barrier, inc=1, device_id=(e, lax.rem(me + i, 64)), device_id_type=MESH)
        return carry

    def greet_ens(i, carry):
        pl.semaphore_signal(barrier, inc=1, device_id=(lax.rem(e + i, 8), me), device_id_type=MESH)
        return carry

    lax.fori_loop(1, 64, greet, 0)
    lax.fori_loop(1, 8, greet_ens, 0)

    def remote(src, dst, j, dev):
        return pltpu.make_async_remote_copy(
            src, dst, ss.at[j], rs.at[j], device_id=dev, device_id_type=MESH
        )

    def all_of(src, dst, j, n):
        return remote(src.at[pl.ds(0, n)], dst.at[pl.ds(0, n)], j, (e, lax.rem(me + 1, 64)))

    for h in range(2):
        for f in range(2):
            t = tok[h, :, f * 384 : (f + 1) * 384]
            lonbuf[f, h] = dot(lon_hi[...], t) + dot(lon_lo[...], t)
    pl.semaphore_wait(barrier, 70)

    def pair(d):
        f, g = lax.div(d, 32), pl.multiple_of(lax.rem(d, 32) * 8, 8)
        return jnp.concatenate([lonbuf[f, 0, pl.ds(g, 8), :], lonbuf[f, 1, pl.ds(g, 8), :]], axis=0)

    def code(d):
        z = pair(d)
        az = jnp.abs(z)
        top = jnp.max(az, axis=0, keepdims=True)
        top = jnp.maximum(jnp.maximum(top[:, :128], top[:, 128:256]), top[:, 256:])
        top = jnp.maximum(top, 1e-30)
        y = jnp.exp2(az * wide(CODE_SPAN / top) - CODE_BASE)
        return jnp.where(z < 0.0, -y, y).astype(BF), top

    def send_tok(i, carry):
        d = lax.rem(me + i, 64)
        y, top = code(d)
        send_t[d] = y
        send_s[d] = top
        remote(send_t.at[d], recv_t.at[me], 0, (e, d)).start()
        remote(send_s.at[d], recv_s.at[me], 1, (e, d)).start()
        return carry

    lax.fori_loop(1, 64, send_tok, 0)
    y, top = code(me)
    recv_t[me] = y
    recv_s[me] = top

    row = iota((256, 384), 0)
    scale = jnp.where((row == 0) | (row == 4), 1.0, 2.0)
    for h in range(2):
        for f in range(2):
            lonbuf[f, h] = dot(lon_hi[...], cot[h, :, f * 384 : (f + 1) * 384]) * scale

    def send_cot(i, carry):
        d = lax.rem(me + i, 64)
        send_c[d] = pair(d).astype(BF)
        remote(send_c.at[d], recv_c.at[me], 2, (e, d)).start()
        return carry

    lax.fori_loop(1, 64, send_cot, 0)
    recv_c[me] = pair(me).astype(BF)

    q, j = iota((192, 768), 0), iota((192, 768), 1)
    jm = jnp.where(j >= 384, j - 384, j)
    inner = jm - 96 * block_of(jm) + jnp.where(j >= 384, 96, 0)
    spread = jnp.where(q == inner, 1.0, 0.0).astype(BF)
    r, j = iota((384, 768), 0), iota((384, 768), 1)
    own = block_of(r) == block_of(jnp.where(j >= 384, j - 384, j))
    here = pl.ds(pl.multiple_of(half * 384, 384), 384)
    v1[...] = jnp.where(own, dot(w1[here, :], spread), 0.0).astype(BF)
    v2[...] = jnp.where(own, dot(w2[here, :], spread), 0.0).astype(BF)

    def bias(ref):
        t = ref[...].astype(F32)
        t = jnp.where(half == 0, t[:, :384], t[:, 384:])
        return t[0:1], t[1:2]

    b1r, b1i = bias(b1)
    b2r, b2i = bias(b2)

    all_of(send_t, recv_t, 0, 63).wait_recv()
    all_of(send_s, recv_s, 1, 63).wait_recv()

    def put_rows(i, x):
        for t in range(3):
            rows[t, pl.ds(pl.multiple_of(i * 16, 16), 16), :] = x[:, 128 * t : 128 * (t + 1)]

    def mode_rows(k):
        return jnp.concatenate([rows[t, pl.ds(k, 256, stride=4), :] for t in range(3)], axis=1)

    def decode(i, carry):
        y = recv_t[i].astype(F32)
        u = (jnp.log2(jnp.abs(y)) + CODE_BASE) * wide(recv_s[i] * (1.0 / CODE_SPAN))
        put_rows(i, jnp.where(y < 0.0, -u, u))
        return carry

    lax.fori_loop(0, 64, decode, 0)
    for k in range(4):
        hi, lo = halves(mode_rows(k))
        xh[k] = hi
        xl[k] = lo

    def mix(x, v, br, bi):
        hi, lo = halves(x)
        t = dot(hi, v[...]) + dot(lo, v[...])
        real = t[:128, :384] - t[128:, 384:] + br
        imag = t[:128, 384:] + t[128:, :384] + bi
        return hi, jnp.concatenate([real, imag], axis=0)

    def forward(k, carry):
        s = dot(lat_hi[...], xh[k]) + dot(lat_hi[...], xl[k]) + dot(lat_lo[...], xh[k])
        hi, pre = mix(s, v1, b1r, b1i)
        spec_b[k] = hi
        hi, pre = mix(jnp.maximum(pre, 0.0), v2, b2r, b2i)
        first_b[k] = hi
        mask_b[k] = jnp.where(jnp.abs(pre) > LEVEL, 1.0, 0.0).astype(BF)
        return carry

    lax.fori_loop(0, 4, forward, 0)

    all_of(send_c, recv_c, 2, 63).wait_recv()

    def unpack(i, carry):
        put_rows(i, recv_c[i].astype(F32))
        return carry

    lax.fori_loop(0, 64, unpack, 0)
    for k in range(4):
        xh[k] = mode_rows(k).astype(BF)

    def back(g, v):
        br, bi = dot_t(g, v[:, :384]), dot_t(g, v[:, 384:])
        return jnp.concatenate([br[:128] + bi[128:], br[128:] - bi[:128]], axis=0)

    def backward(k, carry):
        g2 = jnp.where(mask_b[k].astype(F32) > 0.0, dot(lat_hi[...], xh[k]), 0.0).astype(BF)
        g2_b[k] = g2
        g1 = jnp.where(first_b[k].astype(F32) > 0.0, back(g2, v2), 0.0).astype(BF)
        g1_b[k] = g1
        lonbuf[lax.div(k, 2), lax.rem(k, 2)] = dot(lat_t[...], back(g1, v1).astype(BF))
        return carry

    lax.fori_loop(0, 4, backward, 0)
    for k in range(4):
        for t in range(3):
            rows[t, pl.ds(k, 256, stride=4), :] = lonbuf[k // 2, k % 2, :, 128 * t : 128 * (t + 1)]

    def grad_block(d):
        at = pl.ds(pl.multiple_of(d * 16, 16), 16)
        return jnp.concatenate([rows[t, at, :] for t in range(3)], axis=1).astype(BF)

    def send_grad(i, carry):
        d = lax.rem(me + i, 64)
        send_g[d] = grad_block(d)
        remote(send_g.at[d], recv_g.at[me], 3, (e, d)).start()
        return carry

    lax.fori_loop(1, 64, send_grad, 0)
    recv_g[me] = grad_block(me)

    r1[...] = jnp.zeros_like(r1)
    r2[...] = jnp.zeros_like(r2)
    slot, col = iota((512, 256), 0), iota((512, 256), 1)
    ones = jnp.where((jnp.bitwise_and(slot, 15) == 12) & (col < 128), 1.0, 0.0)

    def outer(left, g):
        lt = (dot_t(place[...], left) + ones).astype(BF)
        swapped = jnp.concatenate([g[128:], -g[:128]], axis=0)
        return dot(lt, g), dot(lt, swapped)

    def weights(k, carry):
        a, b = outer(spec_b[k], g1_b[k])
        r1[:, :384] += a
        r1[:, 384:] += b
        a, b = outer(first_b[k], g2_b[k])
        r2[:, :384] += a
        r2[:, 384:] += b
        return carry

    lax.fori_loop(0, 4, weights, 0)

    def fold(n, part, ref):
        lane, to = iota((384, 384), 0), iota((384, 384), 1)
        total = 0.0
        for p in range(2):
            pick = jnp.where((lane - 96 * n == to - 192 * part - 96 * p) & (block_of(lane) == n), 1.0, 0.0).astype(BF)
            hi, lo = halves(ref[128 * n : 128 * (n + 1), 384 * p : 384 * (p + 1)])
            total = total + dot(hi, pick) + dot(lo, pick)
        return total

    for n in range(4):
        t = (fold(n, 0, r1) + fold(n, 1, r2)) * FACTOR
        send_a[4 * (n // 2) : 4 * (n // 2) + 4, n % 2] = t.reshape(4, 32, 384)

    x = lax.rem(me, 4)
    z = lax.rem(lax.div(me, 4), 4)
    mine = lax.rem(lax.div(me, 16), 2) * 4 + x

    def send_plane(i, carry):
        o = lax.rem(mine + i, 8)
        d = half * 32 + lax.div(o, 4) * 16 + z * 4 + lax.rem(o, 4)
        remote(send_a.at[o], recv_a.at[mine], 4, (e, d)).start()
        return carry

    lax.fori_loop(1, 8, send_plane, 0)
    recv_a[mine] = send_a[mine]
    all_of(send_a, recv_a, 4, 7).wait_recv()
    total = recv_a[0]
    for o in range(1, 8):
        total = total + recv_a[o]
    send_b[...] = total.reshape(4, 16, 384)

    def send_z(i, carry):
        o = lax.rem(z + i, 4)
        remote(send_b.at[o], recv_b.at[z], 5, (e, me + (o - z) * 4)).start()
        return carry

    lax.fori_loop(1, 4, send_z, 0)
    recv_b[z] = send_b[z]
    all_of(send_b, recv_b, 5, 3).wait_recv()
    total = recv_b[0] + recv_b[1] + recv_b[2] + recv_b[3]
    send_e[0] = total

    def send_ens(i, carry):
        remote(send_e.at[0], recv_e.at[e], 6, (lax.rem(e + i, 8), me)).start()
        return carry

    lax.fori_loop(1, 8, send_ens, 0)
    recv_e[e] = total
    all_of(recv_e, recv_e, 6, 7).wait_recv()
    total = recv_e[0]
    for o in range(1, 8):
        total = total + recv_e[o]
    out_w[...] = total

    all_of(send_g, recv_g, 3, 63).wait_recv()
    for f in range(2):
        t = recv_g[32 * f : 32 * (f + 1)].astype(F32)
        for h in range(2):
            g = t[:, 8 * h : 8 * (h + 1), :].reshape(256, 384).astype(BF)
            branch = dot(lon_t[...], g)
            lanes = slice(384 * f, 384 * (f + 1))
            out[h, :, lanes] = (cot[h, :, lanes].astype(F32) + branch).astype(BF)

    all_of(send_t, recv_t, 0, 63).wait_send()
    all_of(send_s, recv_s, 1, 63).wait_send()
    all_of(send_c, recv_c, 2, 63).wait_send()
    all_of(send_g, recv_g, 3, 63).wait_send()
    all_of(send_a, recv_a, 4, 7).wait_send()
    all_of(send_b, recv_b, 5, 3).wait_send()
    all_of(recv_e, recv_e, 6, 7).wait_send()


def shards(tables, tokens, cotangent, w_first, b_first, w_second, b_second):
    blocks = lambda n, kind: pltpu.VMEM((n, 16, 384), kind)
    parts = lambda kind: pltpu.VMEM((4, 256, 384), kind)
    scratch = [
        pltpu.VMEM((2, 2, 256, 384), F32),
        blocks(64, BF), pltpu.VMEM((64, 1, 128), F32), blocks(64, BF), pltpu.VMEM((64, 1, 128), F32),
        blocks(64, BF), blocks(64, BF), blocks(64, BF), blocks(64, BF),
        pltpu.VMEM((3, 1024, 128), F32),
        parts(BF), parts(BF), parts(BF), parts(BF), parts(BF), parts(BF), parts(BF),
        pltpu.VMEM((384, 768), BF), pltpu.VMEM((384, 768), BF),
        pltpu.VMEM((512, 768), F32), pltpu.VMEM((512, 768), F32),
        pltpu.VMEM((8, 2, 32, 384), F32), pltpu.VMEM((8, 2, 32, 384), F32),
        blocks(4, F32), blocks(4, F32), blocks(1, F32), blocks(8, F32),
        pltpu.SemaphoreType.DMA((7,)), pltpu.SemaphoreType.DMA((7,)),
    ]
    spec = pl.BlockSpec(memory_space=pltpu.VMEM)
    field, grads = pl.pallas_call(
        kernel,
        out_shape=(jax.ShapeDtypeStruct((2, 384, 768), BF), jax.ShapeDtypeStruct((16, 384), F32)),
        in_specs=[spec] * 13,
        out_specs=(spec, spec),
        scratch_shapes=scratch,
        name="afno_backward",
        compiler_params=pltpu.CompilerParams(
            collective_id=0, has_side_effects=True, vmem_limit_bytes=48 << 20
        ),
    )(tokens[0], cotangent[0], w_first, b_first, w_second, b_second, *[jnp.asarray(t) for t in tables])
    at = lax.rem(lax.axis_index("sp"), 8) * 12
    sums = grads[12].reshape(2, 2, 96)
    sums = lax.dynamic_slice_in_dim(sums, at, 12, 2)
    return field[None], grads[:12, :192], sums[0], grads[:12, 192:], sums[1]


def solution(mesh):
    return jax.shard_map(
        functools.partial(shards, constants()),
        mesh=mesh,
        in_specs=(P("ens", "sp", None, None), P("ens", "sp", None, None), P(), P(), P(), P()),
        out_specs=(
            P("ens", "sp", None, None),
            P("sp", None),
            P(None, "sp"),
            P("sp", None),
            P(None, "sp"),
        ),
        check_vma=False,
    )
```

time: 766 us -> 153 us (0.20)
  waiting for transfers between devices: 439 us -> 0 us
  Pallas kernels: 0 us -> 140 us
  blocking collectives: 105 us -> 0 us
  starting transfers between devices: 76.7 us -> 0 us
  local copies, waits for them, and re-layouts: 85.3 us -> 11.7 us
  matrix products: 22.5 us -> 0 us
  other arithmetic: 15.9 us -> 0 us
  between operations: 14.7 us -> 0.73 us
    psum x1 -> x0, waiting for transfers between devices: 368 us -> none  [shards(): totals = lax.psum((terms[0], terms[1], terms[2], terms[3]), ('ens', 'sp'))]
    pallas_call x0 -> x1, Pallas kernels: none -> 140 us  [shards(): pl.pallas_call(kernel, out_shape=(jax.ShapeDtypeStruct((2, 384, 768), BF)...]
    psum x1 -> x0, blocking collectives: 105 us -> none  [shards(): totals = lax.psum((terms[0], terms[1], terms[2], terms[3]), ('ens', 'sp'))]
    all_to_all x3 -> x0, starting transfers between devices: 76.7 us -> none  [the longest x1 42.8 us: shards(): lax.all_to_all(grad_lat, 'sp', split_axis=0, concat_axis=2, tiled=True)]
    all_to_all x3 -> x0, waiting for transfers between devices: 71.4 us -> none  [the longest x1 36.6 us: shards(): lax.all_to_all(cot_lon, 'sp', split_axis=2, concat_axis=0, tiled=True)]
    another operation x10 -> x1, local copies, waits for them, and re-layouts: 24 us -> 0.09 us  [shards(): sums = grads[12].reshape(2, 2, 96)]
    dot_general x12 -> x0, matrix products: 22.5 us -> none  [product(): jnp.einsum(form, left, right, precision=lax.Precision.HIGHEST, preferred_...]
    slice x6 -> x2, local copies, waits for them, and re-layouts: 14.5 us -> 0.7 us  [the longest x1 0.68 us: shards(): return (field[None], grads[:12, :192], sums[0], grads[:12, 192:], sums[1])]
  transfers between devices with their start and end apart: 4 -> 0, of which waited for: 3 -> 0; matrix products, arithmetic and copies ran while one was open for 3% -> 0% of each run, Pallas kernels for 0% -> 0%
where the time goes in v1:
time: 153 us; the launch traced here: 152 us
  Pallas kernels  140 us (92%)
  local copies, waits for them, and re-layouts  11.7 us (8%)
    pallas_call x1, Pallas kernels, shards(): pl.pallas_call(kernel, out_shape=(jax.ShapeDtypeStruct((2, 384, 768), BF)...  140 us
    unnamed x25, local copies, waits for them, and re-layouts  10.2 us

profile of v1, /device:TPU:6, one launch (start us, length us, event | category | flops | bytes accessed | tf_op | source)
XLA Modules:
  0.0 152.2 jit_solution(8656777156338947451)
XLA Ops:
  0.6 0.0 copy-start.3
  0.6 0.0 copy-start
  0.7 0.0 copy-start.9
  0.7 0.0 copy-start.10
  0.7 1.2 copy.18.w1
  1.9 1.1 copy.19.w2
  3.0 0.0 copy-done.3
  3.1 0.0 copy-done
  3.1 0.0 copy-done.9
  3.1 0.0 copy-done.10
  3.1 0.0 copy-start.1
  3.1 1.3 copy-done.1
  4.4 0.0 copy-start.2
  4.4 1.0 copy-done.2
  5.4 0.9 copy-done.4
  6.3 0.9 copy-done.5
  7.2 0.9 copy-done.6
  8.1 0.9 copy-done.7
  9.0 0.9 copy-done.8
  9.9 139.8 %afno_backward.1 = (bf16[2,384,768]{2,1,0:T(8,128)(2,1)S(1)}, f32[16,384]{1,0:T(8,128)S(1)}) custom-call(bf16[2,384,768]{2,1,0:T(8,128)(2,1)S(1)} %bitcast.7, bf16[2,384,768]{2,1,0:T(8,128)(2,1)S(1)} %bitcast.8, bf16[768,192]{1,0:T(8,128)(2,1)S(1)} %copy.18.w1, bf16[2,768]{1,0:T(2,128)(2,1)S(1)} %copy-done.9, bf16[768,192]{1,0:T(8,128)(2,1)S(1)} %copy.19.w2, ...), custom_call_target="tpu_custom_call" | custom-call | tf_op jit(solution)/shard_map/afno_backward/pallas_call | solution.py:361
  149.7 0.7 fusion
  150.4 0.1 reshape_squeeze.3
  150.5 0.6 dynamic-slice_bitcast_fusion
  151.2 1.0 copy.21
  (6 shorter events, 0.0 us)
Async XLA Ops:
  0.6 2.4 %copy-start.3 = (bf16[256,384]{1,0:T(8,128)(2,1)S(1)}, bf16[256,384]{1,0:T(8,128)(2,1)}, u32[]{:S(2)}) copy-start(bf16[256,384]{1,0:T(8,128)(2,1)} %constant.28.clone.lon_hi) | copy-start | bytes 589828
  0.6 2.4 %copy-start = (bf16[1,2,384,768]{3,2,1,0:T(8,128)(2,1)S(1)}, bf16[1,2,384,768]{3,2,1,0:T(8,128)(2,1)}, u32[]{:S(2)}) copy-start(bf16[1,2,384,768]{3,2,1,0:T(8,128)(2,1)} %param.13) | copy-start | bytes 3538948
  0.7 2.4 %copy-start.9 = (bf16[2,768]{1,0:T(2,128)(2,1)S(1)}, bf16[2,768]{1,0:T(2,128)(2,1)}, u32[]{:S(2)}) copy-start(bf16[2,768]{1,0:T(2,128)(2,1)} %b1.1) | copy-start | bytes 9220
  0.7 2.4 %copy-start.10 = (bf16[2,768]{1,0:T(2,128)(2,1)S(1)}, bf16[2,768]{1,0:T(2,128)(2,1)}, u32[]{:S(2)}) copy-start(bf16[2,768]{1,0:T(2,128)(2,1)} %b2.1) | copy-start | bytes 9220
  3.1 1.3 copy-start.1
  4.4 1.0 copy-start.2
  5.4 0.9 copy-start.4
  6.3 0.9 copy-start.5
  7.2 0.9 copy-start.6
  8.1 0.9 copy-start.7
  9.0 0.9 copy-start.8

commit v2 on v1

v2 whole, which is shorter than its diff:
```python
import functools

import jax
import jax.numpy as jnp
import ml_dtypes
import numpy as np
from jax import lax
from jax.experimental import pallas as pl
from jax.experimental.pallas import tpu as pltpu
from jax.sharding import PartitionSpec as P

MESH = pl.DeviceIdType.MESH
BF = jnp.bfloat16
F32 = jnp.float32
LEVEL = 0.01
CODE_SPAN = 249.0
CODE_BASE = 124.0
FACTOR = float(131072) ** (-0.5)
WINDOWS = (0, 0, 128, 128)


def constants():
    k = np.arange(128)[:, None]
    w = np.arange(384)[None, :]
    a = 2.0 * np.pi * ((k * w) % 384) / 384.0
    lon = (np.stack([np.cos(a), -np.sin(a)]) / np.sqrt(384.0)).astype(np.float32)
    lon = lon.reshape(2, 32, 4, 384).transpose(1, 0, 2, 3).reshape(256, 384)
    m = np.arange(128)[:, None]
    h = np.arange(128)[None, :]
    b = 2.0 * np.pi * ((m * h) % 128) / 128.0
    c, s = np.cos(b) / np.sqrt(128.0), np.sin(b) / np.sqrt(128.0)
    lat = np.stack([np.stack([c, s], 2), np.stack([-s, c], 2)])
    lat = lat.astype(np.float32).reshape(256, 256)

    def split(t):
        hi = t.astype(ml_dtypes.bfloat16)
        return hi, (t - hi.astype(np.float32)).astype(ml_dtypes.bfloat16)

    lon_hi, lon_lo = split(lon)
    lat_hi, lat_lo = split(lat)
    place = np.zeros((2, 2, 4, 2, 16, 384), np.float32)
    for yy in range(2):
        for z in range(4):
            for x in range(4):
                for r in range(12):
                    place[yy, z // 2, x, z % 2, r, yy * 192 + z * 48 + x * 12 + r] = 1.0
    place = place.reshape(512, 384).astype(ml_dtypes.bfloat16)
    return [lon_hi, lon_lo, np.ascontiguousarray(lon_hi.T), lat_hi, lat_lo, np.ascontiguousarray(lat_hi.T), place]


def dot(a, b):
    return lax.dot_general(a, b, (((1,), (0,)), ((), ())), preferred_element_type=F32)


def dot_t(a, b):
    return lax.dot_general(a, b, (((1,), (1,)), ((), ())), preferred_element_type=F32)


def halves(x):
    hi = x.astype(BF)
    return hi, (x - hi.astype(F32)).astype(BF)


def iota(shape, dim):
    return lax.broadcasted_iota(jnp.int32, shape, dim)


def block_of(i):
    return (i >= 96).astype(jnp.int32) + (i >= 192).astype(jnp.int32) + (i >= 288).astype(jnp.int32)


def wide(s):
    return jnp.concatenate([s, s, s], axis=1)


def kernel(
    tok_a, cot_a, w1_a, b1_a, w2_a, b2_a, lon_hi_a, lon_lo_a, lon_t_a, lat_hi_a, lat_lo_a, lat_t_a, place_a,
    out, out_w,
    tok, cot, w1, b1, w2, b2, lon_hi, lon_lo, lon_t, lat_hi, lat_lo, lat_t, place, load,
    lonbuf, send_t, send_s, recv_t, recv_s, send_cx, recv_cx, send_cy, recv_cy, send_g0, recv_g0, send_g1, recv_g1, middle,
    rows, xh, xl, first_b, mask_b, g1_b, g2_b, v1, v2, left1, left2, pick,
    send_a, recv_a, send_b, recv_b, send_e, recv_e, ss, rs,
):
    pairs = [
        (lon_hi_a, lon_hi), (lon_lo_a, lon_lo), (tok_a, tok), (cot_a, cot), (w1_a, w1), (b1_a, b1), (w2_a, w2),
        (b2_a, b2), (lat_hi_a, lat_hi), (lat_lo_a, lat_lo), (lat_t_a, lat_t), (place_a, place), (lon_t_a, lon_t),
    ]
    loads = [pltpu.make_async_copy(a, b, load.at[n]) for n, (a, b) in enumerate(pairs)]
    for copy in loads:
        copy.start()
    e = lax.axis_index("ens")
    me = lax.axis_index("sp")
    half = lax.div(me, 32)
    barrier = pltpu.get_barrier_semaphore()

    def greet(i, carry):
        pl.semaphore_signal(barrier, inc=1, device_id=(e, lax.rem(me + i, 64)), device_id_type=MESH)
        return carry

    def greet_ens(i, carry):
        pl.semaphore_signal(barrier, inc=1, device_id=(lax.rem(e + i, 8), me), device_id_type=MESH)
        return carry

    lax.fori_loop(1, 64, greet, 0)
    lax.fori_loop(1, 8, greet_ens, 0)
    x = lax.rem(me, 4)
    y = lax.div(me, 16)
    z = lax.rem(lax.div(me, 4), 4)
    core = lax.rem(e, 2)
    mine = core * 8 + lax.rem(y, 2) * 4 + x

    def peer(o):
        j = lax.rem(o, 8)
        return (e - core + lax.div(o, 8), half * 32 + lax.div(j, 4) * 16 + z * 4 + lax.rem(j, 4))

    def greet_core(i, carry):
        o = (1 - core) * 8 + lax.rem(mine + i, 8)
        pl.semaphore_signal(barrier, inc=1, device_id=peer(o), device_id_type=MESH)
        return carry

    lax.fori_loop(1, 8, greet_core, 0)

    def remote(src, dst, j, dev):
        return pltpu.make_async_remote_copy(
            src, dst, ss.at[j], rs.at[j], device_id=dev, device_id_type=MESH
        )

    def all_of(src, dst, j, n):
        return remote(src.at[pl.ds(0, n)], dst.at[pl.ds(0, n)], j, (e, lax.rem(me + 1, 64)))

    for copy in loads[:3]:
        copy.wait()
    for h in range(2):
        for f in range(2):
            t = tok[h, :, f * 384 : (f + 1) * 384]
            lonbuf[f, h] = dot(lon_hi[...], t) + dot(lon_lo[...], t)
    pl.semaphore_wait(barrier, 77)

    def dest(i):
        return lax.rem(me + i, 64)

    def pair(buf, d):
        f, g = lax.div(d, 32), pl.multiple_of(lax.rem(d, 32) * 8, 8)
        return jnp.concatenate([buf[f, 0, pl.ds(g, 8), :], buf[f, 1, pl.ds(g, 8), :]], axis=0)

    def send_tok(i, carry):
        d = dest(i)
        v = pair(lonbuf, d)
        av = jnp.abs(v)
        top = jnp.max(av, axis=0, keepdims=True)
        top = jnp.maximum(jnp.maximum(top[:, :128], top[:, 128:256]), top[:, 256:])
        top = jnp.maximum(top, 1e-30)
        coded = jnp.exp2(av * wide(CODE_SPAN / top) - CODE_BASE)
        send_t[d] = jnp.where(v < 0.0, -coded, coded).astype(BF)
        send_s[d] = top

        @pl.when(d != me)
        def _():
            remote(send_t.at[d], recv_t.at[me], 0, (e, d)).start()
            remote(send_s.at[d], recv_s.at[me], 1, (e, d)).start()

        return carry

    def send_cot(part, i, carry):
        d = dest(i)
        src, dst = (send_cx, recv_cx) if part == 0 else (send_cy, recv_cy)
        v = pair(lonbuf, d)
        src[d] = (v[:, :256] if part == 0 else v[:, 256:]).astype(BF)

        @pl.when(d != me)
        def _():
            remote(src.at[d], dst.at[me], 2 + part, (e, d)).start()

        return carry

    lax.fori_loop(0, 64, send_tok, 0)
    recv_t[me] = send_t[me]
    recv_s[me] = send_s[me]
    loads[3].wait()
    row = iota((256, 384), 0)
    scale = jnp.where((row == 0) | (row == 4), 1.0, 2.0)
    for h in range(2):
        for g in range(2):
            lonbuf[g, h] = dot(lon_hi[...], cot[h, :, g * 384 : (g + 1) * 384]) * scale
    lax.fori_loop(0, 64, functools.partial(send_cot, 0), 0)
    lax.fori_loop(0, 64, functools.partial(send_cot, 1), 0)
    recv_cx[me] = send_cx[me]
    recv_cy[me] = send_cy[me]

    for copy in loads[4:]:
        copy.wait()
    q, j = iota((192, 768), 0), iota((192, 768), 1)
    jm = jnp.where(j >= 384, j - 384, j)
    inner = jm - 96 * block_of(jm) + jnp.where(j >= 384, 96, 0)
    spread = jnp.where(q == inner, 1.0, 0.0).astype(BF)
    r, j = iota((384, 768), 0), iota((384, 768), 1)
    own = block_of(r) == block_of(jnp.where(j >= 384, j - 384, j))

    def diagonal(w):
        t = jnp.where(half == 0, w[:, :384].astype(F32), w[:, 384:].astype(F32)).astype(BF)
        t = lax.dot_general(t, spread, (((0,), (0,)), ((), ())), preferred_element_type=F32)
        return jnp.where(own, t, 0.0).astype(BF)

    v1[...] = diagonal(w1)
    v2[...] = diagonal(w2)

    def bias(ref):
        t = ref[...].astype(F32)
        t = jnp.where(half == 0, t[:, :384], t[:, 384:])
        return t[0:1], t[1:2]

    lane, to = iota((256, 384), 0), iota((256, 384), 1)
    for n in range(4):
        for part in range(4):
            at = 96 * n - WINDOWS[n]
            inside = (lane >= at) & (lane < at + 96)
            pick[n, part] = jnp.where((lane - at == to - 96 * part) & inside, 1.0, 0.0).astype(BF)
    slot, col = iota((512, 256), 0), iota((512, 256), 1)
    ones = jnp.where((jnp.bitwise_and(slot, 15) == 12) & (col < 128), 1.0, 0.0)

    b1r, b1i = bias(b1)
    b2r, b2i = bias(b2)

    all_of(send_t, recv_t, 0, 63).wait_recv()
    all_of(send_s, recv_s, 1, 63).wait_recv()

    def put_rows(i, x):
        for t in range(3):
            rows[t, pl.ds(pl.multiple_of(i * 16, 16), 16), :] = x[:, 128 * t : 128 * (t + 1)]

    def mode_rows(k):
        return jnp.concatenate([rows[t, pl.ds(k, 256, stride=4), :] for t in range(3)], axis=1)

    def decode(i, carry):
        y = recv_t[i].astype(F32)
        u = (jnp.log2(jnp.abs(y)) + CODE_BASE) * wide(recv_s[i] * (1.0 / CODE_SPAN))
        put_rows(i, jnp.where(y < 0.0, -u, u))
        return carry

    lax.fori_loop(0, 64, decode, 0, unroll=4)
    for k in range(4):
        hi, lo = halves(mode_rows(k))
        xh[k] = hi
        xl[k] = lo

    low = iota((256, 128), 1) < 64

    def join(a, b):
        return jnp.concatenate([a[:, :128], jnp.where(low, a[:, 128:], b[:, :128]), b[:, 128:]], axis=1)

    def mix(x, v, br, bi):
        hi, lo = halves(x)

        def window(w, col):
            here = slice(128 * w, 128 * w + 256)
            vw = v[here, 384 * col + 128 * w : 384 * col + 128 * w + 256]
            return dot(hi[:, here], vw) + dot(lo[:, here], vw)

        tr = join(window(0, 0), window(1, 0))
        ti = join(window(0, 1), window(1, 1))
        real = tr[:128] - ti[128:] + br
        imag = ti[:128] + tr[128:] + bi
        return hi, jnp.concatenate([real, imag], axis=0)

    def forward(k, carry):
        s = dot(lat_hi[...], xh[k]) + dot(lat_hi[...], xl[k]) + dot(lat_lo[...], xh[k])
        hi, pre = mix(s, v1, b1r, b1i)
        left1[k] = (dot_t(place[...], hi) + ones).astype(BF)
        hi, pre = mix(jnp.maximum(pre, 0.0), v2, b2r, b2i)
        first_b[k] = hi
        left2[k] = (dot_t(place[...], hi) + ones).astype(BF)
        mask_b[k] = jnp.where(jnp.abs(pre) > LEVEL, 1.0, 0.0).astype(BF)
        return carry

    lax.fori_loop(0, 4, forward, 0)

    def unpack(part, i, carry):
        at = pl.ds(pl.multiple_of(i * 16, 16), 16)
        if part == 0:
            t = recv_cx[i].astype(F32)
            rows[0, at, :] = t[:, :128]
            rows[1, at, :] = t[:, 128:]
        else:
            rows[2, at, :] = recv_cy[i].astype(F32)
        return carry

    def back(g, v, w):
        here = slice(128 * w, 128 * w + 256)
        br = dot_t(g, v[here, here])
        bi = dot_t(g, v[here, 384 + 128 * w : 640 + 128 * w])
        return jnp.concatenate([br[:128] + bi[128:], br[128:] - bi[:128]], axis=0)

    def backward(k, w):
        here = slice(128 * w, 128 * w + 256)
        mine = slice(256 * k, 256 * (k + 1))
        g2 = jnp.where(mask_b[k, :, here].astype(F32) > 0.0, dot(lat_hi[...], xh[k, :, here]), 0.0).astype(BF)
        g2_b[mine, here] = g2
        g1 = jnp.where(first_b[k, :, here].astype(F32) > 0.0, back(g2, v2, w), 0.0).astype(BF)
        if w == 0:
            g1_b[mine, here] = g1
        else:
            g1_b[mine, 128:256] = jnp.where(low, g1_b[mine, 128:256].astype(F32), g1[:, :128].astype(F32)).astype(BF)
            g1_b[mine, 256:] = g1[:, 128:]
        return dot(lat_t[...], back(g1, v1, w).astype(BF))

    def send_grad(part, i, carry):
        d = dest(i)
        at = pl.ds(pl.multiple_of(d * 16, 16), 16)
        src, dst = (send_g0, recv_g0) if part == 0 else (send_g1, recv_g1)
        if part == 0:
            src[d] = rows[0, at, :].astype(BF)
        else:
            src[d] = jnp.concatenate([rows[1, at, :], rows[2, at, :]], axis=1).astype(BF)

        @pl.when(d != me)
        def _():
            remote(src.at[d], dst.at[me], 7 + part, (e, d)).start()

        return carry

    all_of(send_cx, recv_cx, 2, 63).wait_recv()
    lax.fori_loop(0, 64, functools.partial(unpack, 0), 0, unroll=4)
    for k in range(4):
        for t in range(2):
            xh[k, :, 128 * t : 128 * (t + 1)] = rows[t, pl.ds(k, 256, stride=4), :].astype(BF)
    for k in range(4):
        g = backward(k, 0)
        rows[0, pl.ds(k, 256, stride=4), :] = g[:, :128]
        middle[k] = g[:, 128:]
    lax.fori_loop(0, 64, functools.partial(send_grad, 0), 0)
    recv_g0[me] = send_g0[me]

    all_of(send_cy, recv_cy, 3, 63).wait_recv()
    lax.fori_loop(0, 64, functools.partial(unpack, 1), 0, unroll=4)
    for k in range(4):
        xh[k, :, 256:] = rows[2, pl.ds(k, 256, stride=4), :].astype(BF)
    for k in range(4):
        g = backward(k, 1)
        rows[1, pl.ds(k, 256, stride=4), :] = jnp.where(low, middle[k], g[:, :128])
        rows[2, pl.ds(k, 256, stride=4), :] = g[:, 128:]

    def outer(n, left, g):
        lanes = slice(WINDOWS[n], WINDOWS[n] + 256)
        real, imag = 0.0, 0.0
        for k in range(4):
            lt = left[k, 128 * n : 128 * (n + 1), :]
            gr, gi = g[256 * k : 256 * k + 128, lanes], g[256 * k + 128 : 256 * (k + 1), lanes]
            real = real + dot(lt, jnp.concatenate([gr, gi], axis=0))
            imag = imag + dot(lt, jnp.concatenate([gi, -gr], axis=0))
        return real, imag

    for n in range(4):
        total = 0.0
        for part, t in enumerate(outer(n, left1, g1_b) + outer(n, left2, g2_b)):
            hi, lo = halves(t)
            total = total + dot(hi, pick[n, part]) + dot(lo, pick[n, part])
        total = (total * FACTOR).reshape(4, 2, 2, 8, 384)
        for zl in range(2):
            for c in range(2):
                at = c * 8 + 4 * (n // 2)
                send_a[at : at + 4, 2 * (n % 2) + zl] = total[:, zl, c]

    def send_plane(i, carry):
        o = lax.rem(mine + i, 16)
        remote(send_a.at[o], recv_a.at[mine], 4, peer(o)).start()
        return carry

    lax.fori_loop(1, 16, send_plane, 0)
    recv_a[mine] = send_a[mine]
    lax.fori_loop(0, 32, functools.partial(send_grad, 1), 0)
    all_of(send_a, recv_a, 4, 15).wait_recv()
    total = recv_a[0]
    for o in range(1, 16):
        total = total + recv_a[o]
    send_b[...] = total

    def send_z(i, carry):
        o = lax.rem(z + i, 4)
        remote(send_b.at[o], recv_b.at[z], 5, (e, me + (o - z) * 4)).start()
        return carry

    lax.fori_loop(1, 4, send_z, 0)
    recv_b[z] = send_b[z]
    lax.fori_loop(32, 64, functools.partial(send_grad, 1), 0)
    all_of(send_b, recv_b, 5, 3).wait_recv()
    total = recv_b[0] + recv_b[1] + recv_b[2] + recv_b[3]
    send_e[0] = total

    def send_ens(i, carry):
        remote(send_e.at[0], recv_e.at[e], 6, (lax.rem(e + i, 8), me)).start()
        return carry

    lax.fori_loop(1, 8, send_ens, 0)
    recv_e[e] = total
    recv_g1[me] = send_g1[me]

    all_of(send_g0, recv_g0, 7, 63).wait_recv()
    all_of(send_g1, recv_g1, 8, 63).wait_recv()
    for f in range(2):
        at = slice(32 * f, 32 * (f + 1))
        t = jnp.concatenate([recv_g0[at].astype(F32), recv_g1[at].astype(F32)], axis=2)
        for h in range(2):
            g = t[:, 8 * h : 8 * (h + 1), :].reshape(256, 384).astype(BF)
            branch = dot(lon_t[...], g)
            lanes = slice(384 * f, 384 * (f + 1))
            out[h, :, lanes] = (cot[h, :, lanes].astype(F32) + branch).astype(BF)

    all_of(recv_e, recv_e, 6, 7).wait_recv()
    out_w[:8, :] = recv_e[0] + recv_e[2] + recv_e[4] + recv_e[6]
    total = recv_e[1] + recv_e[3] + recv_e[5] + recv_e[7]
    hi, lo = halves(jnp.broadcast_to(total[4:5], (8, 384)))
    lane, to = iota((384, 384), 0), iota((384, 384), 1)
    line = iota((8, 384), 0)
    for part in range(4):
        at = 96 * part + lax.rem(me, 8) * 12
        choose = jnp.where((lane == to + at) & (to < 12), 1.0, 0.0).astype(BF)
        total = jnp.where(line == 4 + part, dot(hi, choose) + dot(lo, choose), total)
    out_w[8:, :] = total

    all_of(send_t, recv_t, 0, 63).wait_send()
    all_of(send_s, recv_s, 1, 63).wait_send()
    all_of(send_cx, recv_cx, 2, 63).wait_send()
    all_of(send_cy, recv_cy, 3, 63).wait_send()
    all_of(send_g0, recv_g0, 7, 63).wait_send()
    all_of(send_g1, recv_g1, 8, 63).wait_send()
    all_of(send_a, recv_a, 4, 15).wait_send()
    all_of(send_b, recv_b, 5, 3).wait_send()
    all_of(recv_e, recv_e, 6, 7).wait_send()


def shards(tables, tokens, cotangent, w_first, b_first, w_second, b_second):
    blocks = lambda n, kind: pltpu.VMEM((n, 16, 384), kind)
    parts = lambda kind: pltpu.VMEM((4, 256, 384), kind)
    loaded = [(2, 384, 768), (2, 384, 768), (192, 768), (2, 768), (192, 768), (2, 768)]
    scratch = [pltpu.VMEM(n, BF) for n in loaded] + [pltpu.VMEM(t.shape, BF) for t in tables]
    scratch += [
        pltpu.SemaphoreType.DMA((13,)),
        pltpu.VMEM((2, 2, 256, 384), F32),
        blocks(64, BF), pltpu.VMEM((64, 1, 128), F32), blocks(64, BF), pltpu.VMEM((64, 1, 128), F32),
        pltpu.VMEM((64, 16, 256), BF), pltpu.VMEM((64, 16, 256), BF), pltpu.VMEM((64, 16, 128), BF), pltpu.VMEM((64, 16, 128), BF),
        pltpu.VMEM((64, 16, 128), BF), pltpu.VMEM((64, 16, 128), BF), pltpu.VMEM((64, 16, 256), BF), pltpu.VMEM((64, 16, 256), BF),
        pltpu.VMEM((4, 256, 128), F32),
        pltpu.VMEM((3, 1024, 128), F32),
        parts(BF), parts(BF), parts(BF), parts(BF),
        pltpu.VMEM((1024, 384), BF), pltpu.VMEM((1024, 384), BF),
        pltpu.VMEM((384, 768), BF), pltpu.VMEM((384, 768), BF),
        pltpu.VMEM((4, 512, 256), BF), pltpu.VMEM((4, 512, 256), BF), pltpu.VMEM((4, 4, 256, 384), BF),
        pltpu.VMEM((16, 4, 8, 384), F32), pltpu.VMEM((16, 4, 8, 384), F32),
        pltpu.VMEM((4, 8, 384), F32), pltpu.VMEM((4, 8, 384), F32),
        pltpu.VMEM((1, 8, 384), F32), pltpu.VMEM((8, 8, 384), F32),
        pltpu.SemaphoreType.DMA((9,)), pltpu.SemaphoreType.DMA((9,)),
    ]
    spec = pl.BlockSpec(memory_space=pltpu.VMEM)
    field, grads = pl.pallas_call(
        kernel,
        out_shape=(jax.ShapeDtypeStruct((2, 384, 768), BF), jax.ShapeDtypeStruct((16, 384), F32)),
        in_specs=[pl.BlockSpec(memory_space=pl.ANY)] * 13,
        out_specs=(spec, spec),
        scratch_shapes=scratch,
        name="afno_backward",
        compiler_params=pltpu.CompilerParams(
            collective_id=0, has_side_effects=True, vmem_limit_bytes=60 << 20
        ),
    )(tokens[0], cotangent[0], w_first.T, b_first, w_second.T, b_second, *[jnp.asarray(t) for t in tables])
    return field[None], grads[:12, :192], grads[12:14, :12], grads[:12, 192:], grads[14:, :12]


def solution(mesh):
    return jax.shard_map(
        functools.partial(shards, constants()),
        mesh=mesh,
        in_specs=(P("ens", "sp", None, None), P("ens", "sp", None, None), P(), P(), P(), P()),
        out_specs=(
            P("ens", "sp", None, None),
            P("sp", None),
            P(None, "sp"),
            P("sp", None),
            P(None, "sp"),
        ),
        check_vma=False,
    )
```

time: 153 us -> 144 us (0.941); the launches traced: 152 us -> 142 us
  local copies, waits for them, and re-layouts: 11.7 us -> 5.16 us
  Pallas kernels: 140 us -> 136 us
    unnamed x25 -> x1, local copies, waits for them, and re-layouts: 10.2 us -> 2.36 us
    pallas_call x1, Pallas kernels: 140 us -> 136 us  [shards(): pl.pallas_call(kernel, out_shape=(jax.ShapeDtypeStruct((2, 384, 768), BF)...]
    slice x2, local copies, waits for them, and re-layouts: 0.7 us -> 2.8 us  [the longest x1 1.47 us: shards(): grads[:12, 192:]]
where the time goes in v2:
time: 144 us; the launch traced here: 142 us
  Pallas kernels  136 us (94%)
  local copies, waits for them, and re-layouts  5.16 us (4%)
    pallas_call x1, Pallas kernels, shards(): pl.pallas_call(kernel, out_shape=(jax.ShapeDtypeStruct((2, 384, 768), BF)...  136 us

profile of v2, /device:TPU:6, one launch (start us, length us, event | category | flops | bytes accessed | tf_op | source)
XLA Modules:
  0.0 141.5 jit_solution(1066609610782178748)
XLA Ops:
  0.6 135.7 %afno_backward.1 = (bf16[2,384,768]{2,1,0:T(8,128)(2,1)}, f32[16,384]{1,0:T(8,128)}) custom-call(bf16[2,384,768]{2,1,0:T(8,128)(2,1)} %bitcast.5, bf16[2,384,768]{2,1,0:T(8,128)(2,1)} %bitcast.6, bf16[192,768]{1,0:T(8,128)(2,1)} %bitcast.8, bf16[2,768]{1,0:T(2,128)(2,1)} %b1_a.1, bf16[192,768]{1,0:T(8,128)(2,1)} %bitcast.9, bf16[2,768]{1,0:T(2,128)(2,1)} %b2_a.1, ...), custom_call_target="tpu_custom_call" | custom-call | tf_op jit(solution)/shard_map/afno_backward/pallas_call | solution.py:454
  136.3 1.3 fusion
  137.7 1.5 %fusion.1 = (f32[12,192]{1,0:T(8,128)}, f32[12,192]{1,0:T(8,128)}) fusion(f32[16,384]{1,0:T(8,128)} %get-tuple-element.8), kind=kLoop, calls=%fused_computation.1 | loop fusion | bytes 36864 | tf_op jit(solution)/shard_map/slice | solution.py:465
  139.2 2.4 %copy.19 = bf16[1,2,384,768]{3,2,1,0:T(8,128)(2,1)} copy(bf16[1,2,384,768]{3,2,1,0:T(8,128)(2,1)} %bitcast.7) | data formatting | bytes 2359296

commit v3 on v2

--- a/solution.py
+++ b/solution.py
@@ -45,7 +45,7 @@
                 for r in range(12):
                     place[yy, z // 2, x, z % 2, r, yy * 192 + z * 48 + x * 12 + r] = 1.0
     place = place.reshape(512, 384).astype(ml_dtypes.bfloat16)
-    return [lon_hi, lon_lo, np.ascontiguousarray(lon_hi.T), lat_hi, lat_lo, np.ascontiguousarray(lat_hi.T), place]
+    return [lon_hi, lon_lo, lat_hi, lat_lo, np.ascontiguousarray(lat_hi.T), place], np.ascontiguousarray(lon_hi.T)
 
 
 def dot(a, b):
@@ -74,16 +74,16 @@
 
 
 def kernel(
-    tok_a, cot_a, w1_a, b1_a, w2_a, b2_a, lon_hi_a, lon_lo_a, lon_t_a, lat_hi_a, lat_lo_a, lat_t_a, place_a,
-    out, out_w,
-    tok, cot, w1, b1, w2, b2, lon_hi, lon_lo, lon_t, lat_hi, lat_lo, lat_t, place, load,
-    lonbuf, send_t, send_s, recv_t, recv_s, send_cx, recv_cx, send_cy, recv_cy, send_g0, recv_g0, send_g1, recv_g1, middle,
+    tok_a, cot_a, w1_a, b1_a, w2_a, b2_a, lon_hi_a, lon_lo_a, lat_hi_a, lat_lo_a, lat_t_a, place_a,
+    recv_g0, recv_g1, out_w,
+    tok, cot, w1, b1, w2, b2, lon_hi, lon_lo, lat_hi, lat_lo, lat_t, place, load,
+    lonbuf, send_t, send_s, recv_t, recv_s, send_cx, recv_cx, send_cy, recv_cy, send_g0, send_g1, middle,
     rows, xh, xl, first_b, mask_b, g1_b, g2_b, v1, v2, left1, left2, pick,
     send_a, recv_a, send_b, recv_b, send_e, recv_e, ss, rs,
 ):
     pairs = [
         (lon_hi_a, lon_hi), (lon_lo_a, lon_lo), (tok_a, tok), (cot_a, cot), (w1_a, w1), (b1_a, b1), (w2_a, w2),
-        (b2_a, b2), (lat_hi_a, lat_hi), (lat_lo_a, lat_lo), (lat_t_a, lat_t), (place_a, place), (lon_t_a, lon_t),
+        (b2_a, b2), (lat_hi_a, lat_hi), (lat_lo_a, lat_lo), (lat_t_a, lat_t), (place_a, place),
     ]
     loads = [pltpu.make_async_copy(a, b, load.at[n]) for n, (a, b) in enumerate(pairs)]
     for copy in loads:
@@ -328,7 +328,8 @@
         rows[0, pl.ds(k, 256, stride=4), :] = g[:, :128]
         middle[k] = g[:, 128:]
     lax.fori_loop(0, 64, functools.partial(send_grad, 0), 0)
-    recv_g0[me] = send_g0[me]
+    own0 = pltpu.make_async_copy(send_g0.at[me], recv_g0.at[me], load.at[12])
+    own0.start()
 
     all_of(send_cy, recv_cy, 3, 63).wait_recv()
     lax.fori_loop(0, 64, functools.partial(unpack, 1), 0, unroll=4)
@@ -392,18 +393,8 @@
 
     lax.fori_loop(1, 8, send_ens, 0)
     recv_e[e] = total
-    recv_g1[me] = send_g1[me]
-
-    all_of(send_g0, recv_g0, 7, 63).wait_recv()
-    all_of(send_g1, recv_g1, 8, 63).wait_recv()
-    for f in range(2):
-        at = slice(32 * f, 32 * (f + 1))
-        t = jnp.concatenate([recv_g0[at].astype(F32), recv_g1[at].astype(F32)], axis=2)
-        for h in range(2):
-            g = t[:, 8 * h : 8 * (h + 1), :].reshape(256, 384).astype(BF)
-            branch = dot(lon_t[...], g)
-            lanes = slice(384 * f, 384 * (f + 1))
-            out[h, :, lanes] = (cot[h, :, lanes].astype(F32) + branch).astype(BF)
+    own1 = pltpu.make_async_copy(send_g1.at[me], recv_g1.at[me], load.at[13])
+    own1.start()
 
     all_of(recv_e, recv_e, 6, 7).wait_recv()
     out_w[:8, :] = recv_e[0] + recv_e[2] + recv_e[4] + recv_e[6]
@@ -417,6 +408,10 @@
         total = jnp.where(line == 4 + part, dot(hi, choose) + dot(lo, choose), total)
     out_w[8:, :] = total
 
+    own0.wait()
+    own1.wait()
+    all_of(send_g0, recv_g0, 7, 63).wait_recv()
+    all_of(send_g1, recv_g1, 8, 63).wait_recv()
     all_of(send_t, recv_t, 0, 63).wait_send()
     all_of(send_s, recv_s, 1, 63).wait_send()
     all_of(send_cx, recv_cx, 2, 63).wait_send()
@@ -428,17 +423,28 @@
     all_of(recv_e, recv_e, 6, 7).wait_send()
 
 
-def shards(tables, tokens, cotangent, w_first, b_first, w_second, b_second):
+def finish(cot, first, second, sums, lon_t, out, w1, b1, w2, b2):
+    t = jnp.concatenate([first[...].astype(F32), second[...].astype(F32)], axis=2)
+    for h in range(2):
+        g = t[:, 8 * h : 8 * (h + 1), :].reshape(256, 384).astype(BF)
+        out[h] = (cot[h].astype(F32) + dot(lon_t[...], g)).astype(BF)
+    w1[...] = sums[:12, :192]
+    w2[...] = sums[:12, 192:]
+    b1[...] = sums[12:14, :12]
+    b2[...] = sums[14:, :12]
+
+
+def shards(tables, lon_t, tokens, cotangent, w_first, b_first, w_second, b_second):
     blocks = lambda n, kind: pltpu.VMEM((n, 16, 384), kind)
     parts = lambda kind: pltpu.VMEM((4, 256, 384), kind)
     loaded = [(2, 384, 768), (2, 384, 768), (192, 768), (2, 768), (192, 768), (2, 768)]
     scratch = [pltpu.VMEM(n, BF) for n in loaded] + [pltpu.VMEM(t.shape, BF) for t in tables]
     scratch += [
-        pltpu.SemaphoreType.DMA((13,)),
+        pltpu.SemaphoreType.DMA((14,)),
         pltpu.VMEM((2, 2, 256, 384), F32),
         blocks(64, BF), pltpu.VMEM((64, 1, 128), F32), blocks(64, BF), pltpu.VMEM((64, 1, 128), F32),
         pltpu.VMEM((64, 16, 256), BF), pltpu.VMEM((64, 16, 256), BF), pltpu.VMEM((64, 16, 128), BF), pltpu.VMEM((64, 16, 128), BF),
-        pltpu.VMEM((64, 16, 128), BF), pltpu.VMEM((64, 16, 128), BF), pltpu.VMEM((64, 16, 256), BF), pltpu.VMEM((64, 16, 256), BF),
+        pltpu.VMEM((64, 16, 128), BF), pltpu.VMEM((64, 16, 256), BF),
         pltpu.VMEM((4, 256, 128), F32),
         pltpu.VMEM((3, 1024, 128), F32),
         parts(BF), parts(BF), parts(BF), parts(BF),
@@ -450,24 +456,46 @@
         pltpu.VMEM((1, 8, 384), F32), pltpu.VMEM((8, 8, 384), F32),
         pltpu.SemaphoreType.DMA((9,)), pltpu.SemaphoreType.DMA((9,)),
     ]
-    spec = pl.BlockSpec(memory_space=pltpu.VMEM)
-    field, grads = pl.pallas_call(
+    spec = pl.BlockSpec(memory_space=pl.ANY)
+    first, second, sums = pl.pallas_call(
         kernel,
-        out_shape=(jax.ShapeDtypeStruct((2, 384, 768), BF), jax.ShapeDtypeStruct((16, 384), F32)),
-        in_specs=[pl.BlockSpec(memory_space=pl.ANY)] * 13,
-        out_specs=(spec, spec),
+        out_shape=(
+            jax.ShapeDtypeStruct((64, 16, 128), BF),
+            jax.ShapeDtypeStruct((64, 16, 256), BF),
+            jax.ShapeDtypeStruct((16, 384), F32),
+        ),
+        in_specs=[spec] * 12,
+        out_specs=(spec, spec, pl.BlockSpec(memory_space=pltpu.VMEM)),
         scratch_shapes=scratch,
         name="afno_backward",
         compiler_params=pltpu.CompilerParams(
             collective_id=0, has_side_effects=True, vmem_limit_bytes=60 << 20
         ),
     )(tokens[0], cotangent[0], w_first.T, b_first, w_second.T, b_second, *[jnp.asarray(t) for t in tables])
-    return field[None], grads[:12, :192], grads[12:14, :12], grads[:12, 192:], grads[14:, :12]
+    whole = lambda *shape: pl.BlockSpec(shape, lambda f: (0,) * len(shape))
+    field = lambda: pl.BlockSpec((2, 384, 384), lambda f: (0, 0, f))
+    part = lambda lanes: pl.BlockSpec((32, 16, lanes), lambda f: (f, 0, 0))
+    out, w1, b1, w2, b2 = pl.pallas_call(
+        finish,
+        grid=(2,),
+        out_shape=(
+            jax.ShapeDtypeStruct((2, 384, 768), BF),
+            jax.ShapeDtypeStruct((12, 192), F32),
+            jax.ShapeDtypeStruct((2, 12), F32),
+            jax.ShapeDtypeStruct((12, 192), F32),
+            jax.ShapeDtypeStruct((2, 12), F32),
+        ),
+        in_specs=[field(), part(128), part(256), whole(16, 384), whole(384, 256)],
+        out_specs=(field(), whole(12, 192), whole(2, 12), whole(12, 192), whole(2, 12)),
+        name="finish",
+        compiler_params=pltpu.CompilerParams(vmem_limit_bytes=60 << 20),
+    )(cotangent[0], first, second, sums, jnp.asarray(lon_t))
+    return out[None], w1, b1, w2, b2
 
 
 def solution(mesh):
     return jax.shard_map(
-        functools.partial(shards, constants()),
+        functools.partial(shards, *constants()),
         mesh=mesh,
         in_specs=(P("ens", "sp", None, None), P("ens", "sp", None, None), P(), P(), P(), P()),
         out_specs=(

time: 144 us -> 140 us (0.972)
  local copies, waits for them, and re-layouts: 5.16 us -> 0 us
  Pallas kernels: 136 us -> 138 us
    slice x2 -> x0, local copies, waits for them, and re-layouts: 2.8 us -> none  [the longest x1 1.47 us: shards(): grads[:12, 192:]]
    unnamed x1 -> x0, local copies, waits for them, and re-layouts: 2.36 us -> none
    pallas_call x1 -> x2, Pallas kernels: 136 us -> 138 us  [the longest x1 135 us: shards(): pl.pallas_call(kernel, out_shape=(jax.ShapeDtypeStruct((64, 16, 128), BF)...]
where the time goes in v3:
time: 140 us; the launch traced here: 138 us
  Pallas kernels  138 us (99%)
    pallas_call x1, Pallas kernels, shards(): pl.pallas_call(kernel, out_shape=(jax.ShapeDtypeStruct((64, 16, 128), BF)...  135 us
    pallas_call x1, Pallas kernels, shards(): pl.pallas_call(finish, grid=(2,), out_shape=(jax.ShapeDtypeStruct((2, 384...  2.94 us

profile of v3, /device:TPU:6, one launch (start us, length us, event | category | flops | bytes accessed | tf_op | source)
XLA Modules:
  0.0 138.4 jit_solution(13631835727126907278)
XLA Ops:
  0.6 134.8 %afno_backward.1 = (bf16[64,16,128]{2,1,0:T(8,128)(2,1)}, bf16[64,16,256]{2,1,0:T(8,128)(2,1)}, f32[16,384]{1,0:T(8,128)}) custom-call(bf16[2,384,768]{2,1,0:T(8,128)(2,1)} %bitcast.7, bf16[2,384,768]{2,1,0:T(8,128)(2,1)} %bitcast.5, bf16[192,768]{1,0:T(8,128)(2,1)} %bitcast.8, bf16[2,768]{1,0:T(2,128)(2,1)} %b1_a.1, bf16[192,768]{1,0:T(8,128)(2,1)} %bitcast.9, ...), custom_call_target="tpu_custom_call" | custom-call | tf_op jit(solution)/shard_map/afno_backward/pallas_call | solution.py:460
  135.4 2.9 %finish.1 = (bf16[2,384,768]{2,1,0:T(8,128)(2,1)}, f32[12,192]{1,0:T(8,128)}, f32[2,12]{1,0:T(2,128)}, f32[12,192]{1,0:T(8,128)}, f32[2,12]{1,0:T(2,128)}) custom-call(bf16[2,384,768]{2,1,0:T(8,128)(2,1)} %bitcast.6, bf16[64,16,128]{2,1,0:T(8,128)(2,1)} %get-tuple-element.13.first, bf16[64,16,256]{2,1,0:T(8,128)(2,1)} %get-tuple-element.14.second, ...), custom_call_target="tpu_custom_call" | custom-call | tf_op jit(solution)/shard_map/finish/pallas_call | solution.py:478

commit v4 on v3

--- a/solution.py
+++ b/solution.py
@@ -137,7 +137,7 @@
     pl.semaphore_wait(barrier, 77)
 
     def dest(i):
-        return lax.rem(me + i, 64)
+        return lax.rem(me + i * (1 + 62 * core), 64)
 
     def pair(buf, d):
         f, g = lax.div(d, 32), pl.multiple_of(lax.rem(d, 32) * 8, 8)

time: 140 us -> 139 us (level)
  the two profiles are of different devices: /device:TPU:6 before, /device:TPU:33 now
where the time goes in v4:
time: 139 us
  Pallas kernels  138 us (99%)
    pallas_call x1, Pallas kernels, shards(): pl.pallas_call(kernel, out_shape=(jax.ShapeDtypeStruct((64, 16, 128), BF)...  135 us
    pallas_call x1, Pallas kernels, shards(): pl.pallas_call(finish, grid=(2,), out_shape=(jax.ShapeDtypeStruct((2, 384...  2.94 us

profile of v4, /device:TPU:33, one launch (start us, length us, event | category | flops | bytes accessed | tf_op | source)
XLA Modules:
  0.0 138.5 jit_solution(18129504104540640238)
XLA Ops:
  0.6 134.9 %afno_backward.1 = (bf16[64,16,128]{2,1,0:T(8,128)(2,1)}, bf16[64,16,256]{2,1,0:T(8,128)(2,1)}, f32[16,384]{1,0:T(8,128)}) custom-call(bf16[2,384,768]{2,1,0:T(8,128)(2,1)} %bitcast.7, bf16[2,384,768]{2,1,0:T(8,128)(2,1)} %bitcast.5, bf16[192,768]{1,0:T(8,128)(2,1)} %bitcast.8, bf16[2,768]{1,0:T(2,128)(2,1)} %b1_a.1, bf16[192,768]{1,0:T(8,128)(2,1)} %bitcast.9, ...), custom_call_target="tpu_custom_call" | custom-call | tf_op jit(solution)/shard_map/afno_backward/pallas_call | solution.py:460
  135.6 2.9 %finish.1 = (bf16[2,384,768]{2,1,0:T(8,128)(2,1)}, f32[12,192]{1,0:T(8,128)}, f32[2,12]{1,0:T(2,128)}, f32[12,192]{1,0:T(8,128)}, f32[2,12]{1,0:T(2,128)}) custom-call(bf16[2,384,768]{2,1,0:T(8,128)(2,1)} %bitcast.6, bf16[64,16,128]{2,1,0:T(8,128)(2,1)} %get-tuple-element.13.first, bf16[64,16,256]{2,1,0:T(8,128)(2,1)} %get-tuple-element.14.second, ...), custom_call_target="tpu_custom_call" | custom-call | tf_op jit(solution)/shard_map/finish/pallas_call | solution.py:478
